TPU v7x, 32 devices: a whole 2x2x4 slice. The times are simulated.
32 devices in a mesh: gx: 8 (over z, y), gy: 4 (over x, core).
Axes of the slice: x: 2, y: 2, z: 4, core: 2. Of those that a mesh axis runs over, the one named last changes fastest.
Arguments:
- cell_means: float32 [30, 32, 16, 128], P(None, 'gx', 'gy'), may hold values from 0 to 1
- diffusion: float32 [32, 16, 128], P('gx', 'gy'), may hold values from 0.02 to 0.15
- mix_rate: float32 [32, 16, 128], P('gx', 'gy'), may hold values from 0.05 to 3
- send_lists: int32 [32, 32, 128], P(('gx', 'gy')), may hold values from 0 to 2047
- compositions: float32 [30, 131072], P(None, ('gx', 'gy')), may hold values from 0 to 1
- weights: float32 [131072], P(('gx', 'gy')), may hold values from 0.5 to 2
- particle_slots: int32 [131072], P(('gx', 'gy')), may hold values from 0 to 4095
- partners: int32 [131072], P(('gx', 'gy')), may hold values from 0 to 4095
Outputs:
- new_means: float32 [30, 32, 16, 128], P(None, 'gx', 'gy')
- new_compositions: float32 [30, 131072], P(None, ('gx', 'gy'))
Inputs may be any that keep to these rules, and one draw needn't show every extreme that they name: particle_slots = s * 128 + r names slot r of the list that tile s sends to the particle's device.
All inputs are finite; a program needn't handle non-finite values.
Results may differ from a plain program's by a relative error of at most 0.00002.
Values sent between devices are 32-bit elements; how exact they have to be, the bound alone decides.
A program may use at most 64 MiB of HBM per device.

v0:
```python
import functools

import jax
import jax.numpy as jnp
from jax import lax
from jax.experimental import pallas as pl
from jax.experimental.pallas import tpu as pltpu
from jax.sharding import PartitionSpec as P

PAIR_RATE = 0.3
LANES = 128
ROWS = 32
GROUPS = ROWS // 8
PLANE = 8
F32 = jnp.float32
BF16 = jnp.bfloat16


def pick(table, count, index, start=0, sums=None):
    lane = jnp.broadcast_to(index & (LANES - 1), (8, LANES))
    chunk = jnp.broadcast_to(index >> 7, (8, LANES))
    if sums is None:
        sums = tuple(jnp.zeros((8, LANES), F32) for _ in range(GROUPS))

    def step(at, sums):
        mask = chunk == at
        return tuple(
            jnp.where(
                mask,
                jnp.take_along_axis(
                    table[at, 8 * g : 8 * g + 8, :], lane, axis=1, mode="promise_in_bounds"
                ),
                total,
            )
            for g, total in enumerate(sums)
        )

    return lax.fori_loop(start, start + count, step, sums, unroll=min(count, 16))


def stencil(cells, halo, diffusion, fields, rows_x, rows_y):
    lane = lax.broadcasted_iota(jnp.int32, (ROWS, LANES), 1)
    for x in range(rows_x):
        for y in range(rows_y):
            mid = cells[x, y]
            total = cells[x + 1, y] if x + 1 < rows_x else halo[1, y]
            total = total + (cells[x - 1, y] if x else halo[0, y])
            total = total + (cells[x, y + 1] if y + 1 < rows_y else halo[3, x])
            total = total + (cells[x, y - 1] if y else halo[2, x])
            total = total + jnp.where(lane < LANES - 1, pltpu.roll(mid, LANES - 1, 1), 0.0)
            total = total + jnp.where(lane > 0, pltpu.roll(mid, 1, 1), 0.0)
            j = x * rows_y + y
            fields[j] = mid + diffusion[j : j + 1, :] * (total - 6.0 * mid)


def scatter_block(group, hot, high, low, left, acc, groups):
    width = group.shape[1]
    group = jnp.broadcast_to(group.astype(F32).astype(BF16), (ROWS, width))
    for g in range(groups):
        mask = group == jnp.array(g, BF16)
        zero = jnp.zeros((ROWS, width), BF16)
        left[2 * g * ROWS : (2 * g + 1) * ROWS, :] = jnp.where(mask, high, zero)
        left[(2 * g + 1) * ROWS : (2 * g + 2) * ROWS, :] = jnp.where(mask, low, zero)
    acc[...] += lax.dot_general(
        left[...], hot, (((1,), (1,)), ((), ())), preferred_element_type=F32
    )


def hot_rows(index):
    place = lax.broadcasted_iota(jnp.int32, (256, index.shape[1]), 0)
    return jnp.where(place == (index & 255), 1.0, 0.0).astype(BF16)


def acc_row(acc, j):
    g, half = j // 2, (j % 2) * LANES
    return (
        acc[2 * g * ROWS : (2 * g + 1) * ROWS, half : half + LANES]
        + acc[(2 * g + 1) * ROWS : (2 * g + 2) * ROWS, half : half + LANES]
    )


def load_cells(means, cells, rows_x, rows_y):
    species = means.shape[0] // (rows_x * rows_y)
    for x in range(rows_x):
        for y in range(rows_y):
            j = x * rows_y + y
            cells[x, y, 0:species, :] = means[pl.ds(j, species, stride=rows_x * rows_y), :]
            cells[x, y, species:ROWS, :] = jnp.zeros((ROWS - species, LANES), F32)


def gather_pairs(compositions, partners, table, parts, pair):
    species, particles = compositions.shape
    groups = particles // 256
    for h in range(groups):
        values = compositions[:, h * 256 : (h + 1) * 256]
        values = jnp.concatenate([values, jnp.zeros((ROWS - species, 256), F32)], 0)
        first = values.astype(BF16)
        table[h * ROWS : (h + 1) * ROWS, 0:256] = first
        table[h * ROWS : (h + 1) * ROWS, 256:512] = (values - first.astype(F32)).astype(BF16)

    def body(k, _):
        index = jnp.concatenate([partners[pl.ds(2 * k + i, 1), :] for i in range(2)], 1)
        place = lax.broadcasted_iota(jnp.int32, (256, 256), 0)
        hot = jnp.where(place == (index & 255), 1.0, 0.0).astype(BF16)
        hot = jnp.concatenate([hot, hot], 0)
        parts[...] = jnp.dot(table[...], hot, preferred_element_type=F32)
        group = jnp.broadcast_to(index >> 8, (ROWS, 256))
        total = jnp.zeros((ROWS, 256), F32)
        for h in range(groups):
            total = jnp.where(group == h, parts[h * ROWS : (h + 1) * ROWS, :], total)
        at = pl.multiple_of(k * 256, 256)
        pair[0:species, pl.ds(at, 256)] = PAIR_RATE * (
            compositions[:, pl.ds(at, 256)] - total[:species]
        )
        return 0

    lax.fori_loop(0, particles // 256, body, 0)


def whole_kernel(
    nx, ny, rows_x, rows_y, *refs
):
    inputs, (out, new_out), refs = refs[:8], refs[8:10], refs[10:]
    staged, refs = refs[:8], refs[8:]
    means, diffusion, rate, lists, compositions, weights, slots, partners = staged
    (
        new, cells, halo, fields, outgoing, received, local, moments, returned,
        table, parts, pair, high, low, hot1, left1, acc1, left2, acc2,
        in_sems, out_sem, halo_send, halo_recv, go_send, go_recv, back_send, back_recv,
    ) = refs
    tiles = nx * ny
    planes = tiles // PLANE
    count = rows_x * rows_y
    species = compositions.shape[0]
    blocks = slots.shape[0]
    gx, gy = lax.axis_index("gx"), lax.axis_index("gy")
    me = gx * ny + gy
    plane, inner = lax.div(me, PLANE), lax.rem(me, PLANE)

    def place(d):
        return (lax.div(d, ny), lax.rem(d, ny))

    loads = [
        pltpu.make_async_copy(inputs[i], staged[i], in_sems.at[i]) for i in range(8)
    ]
    for i in (0, 1, 2, 4, 7, 3, 6, 5):
        loads[i].start()

    barrier = pltpu.get_barrier_semaphore()

    def greet(k, _):
        d = lax.rem(me + k, tiles)
        pl.semaphore_signal(
            barrier, inc=1, device_id=place(d), device_id_type=pl.DeviceIdType.MESH
        )
        return 0

    lax.fori_loop(1, tiles, greet, 0)

    loads[0].wait()
    for x in range(rows_x):
        for y in range(rows_y):
            j = x * rows_y + y
            cells[x, y, 0:species, :] = means[pl.ds(j, species, stride=count), :]
            cells[x, y, species:ROWS, :] = jnp.zeros((ROWS - species, LANES), F32)

    pl.semaphore_wait(barrier, tiles - 1)

    def halo_copy(i):
        source, length, target = (
            (cells.at[rows_x - 1], rows_y, (gx + 1, gy)),
            (cells.at[0], rows_y, (gx - 1, gy)),
            (cells.at[:, rows_y - 1], rows_x, (gx, gy + 1)),
            (cells.at[:, 0], rows_x, (gx, gy - 1)),
        )[i]
        return pltpu.make_async_remote_copy(
            src_ref=source,
            dst_ref=halo.at[i, 0:length],
            send_sem=halo_send.at[i],
            recv_sem=halo_recv.at[i],
            device_id=target,
            device_id_type=pl.DeviceIdType.MESH,
        )

    sends = (gx < nx - 1, gx > 0, gy < ny - 1, gy > 0)
    receives = (gx > 0, gx < nx - 1, gy > 0, gy < ny - 1)
    for i in range(4):

        @pl.when(sends[i])
        def _(i=i):
            halo_copy(i).start()

        @pl.when(jnp.logical_not(receives[i]))
        def _(i=i):
            halo[i] = jnp.zeros(halo.shape[1:], F32)

    loads[4].wait()
    loads[7].wait()
    gather_pairs(compositions, partners, table, parts, pair)
    for i in (1, 2, 3, 5, 6):
        loads[i].wait()
    for b in range(0, blocks, 4):
        index = jnp.concatenate([slots[b + i : b + i + 1, :] for i in range(4)], 1)
        hot1[:, b * LANES : (b + 4) * LANES] = hot_rows(index)
    local[...] = jnp.zeros(local.shape, F32)

    for i in range(4):

        @pl.when(receives[i])
        def _(i=i):
            halo_copy(i).wait_recv()

    stencil(cells, halo, diffusion, fields, rows_x, rows_y)
    blend = 1.0 - jnp.exp(-rate[...])
    for j in range(count):
        fields[j, species : species + 1, :] = blend[j : j + 1, :]

    def copy_of(buffers, sems, source, d, target):
        return pltpu.make_async_remote_copy(
            src_ref=buffers[0].at[d, 0 : species + 1],
            dst_ref=buffers[1].at[source, 0 : species + 1],
            send_sem=sems[0].at[d],
            recv_sem=sems[1].at[source],
            device_id=place(target),
            device_id_type=pl.DeviceIdType.MESH,
        )

    go = (outgoing, received), (go_send, go_recv)
    back = (moments, returned), (back_send, back_recv)

    def fill(d, buffer, row):
        found = pick(fields, count, lists[pl.ds(d, 1), :])
        for g in range(GROUPS):
            buffer[row, 8 * g : 8 * g + 8, :] = found[g]

    def send_plane(there, first):
        def body(i, _):
            d = there * PLANE + lax.rem(inner + i, PLANE)
            fill(d, outgoing, d)
            copy_of(*go, me, d, d).start()
            return 0

        lax.fori_loop(first, PLANE, body, 0)

    def far_first(step):
        half = planes // 2
        lax.fori_loop(half, planes, lambda k, _: (step(k), 0)[1], 0)
        lax.fori_loop(1, half, lambda k, _: (step(half - k), 0)[1], 0)

    far_first(lambda k: send_plane(lax.rem(plane + k, planes), 0))
    fill(me, received, me)
    send_plane(plane, 1)

    def wait_plane(which, there, first):
        def body(i, _):
            s = there * PLANE + lax.rem(inner + i, PLANE)
            copy_of(*which, s, s, s).wait_recv()
            return 0

        lax.fori_loop(first, PLANE, body, 0)

    per = left1.shape[1]

    def work(there, first):
        wait_plane(go, there, first)

        def body(b, _):
            index = slots[pl.ds(b, 1), :]
            lane = jnp.broadcast_to(index & (LANES - 1), (8, LANES))
            chunk = jnp.broadcast_to((index >> 7) - there * PLANE, (8, LANES))
            sums = [local[b, 8 * g : 8 * g + 8, :] for g in range(GROUPS)]
            for i in range(PLANE):
                mask = chunk == i
                for g in range(GROUPS):
                    rows = received[there * PLANE + i, 8 * g : 8 * g + 8, :]
                    found = jnp.take_along_axis(rows, lane, axis=1, mode="promise_in_bounds")
                    sums[g] = jnp.where(mask, found, sums[g])
            for g in range(GROUPS):
                local[b, 8 * g : 8 * g + 8, :] = sums[g]
            at = pl.multiple_of(b * LANES, LANES)
            cell = jnp.concatenate(sums, 0)
            mine = compositions[:, pl.ds(at, LANES)]
            fresh = mine - cell[species : species + 1, :] * (mine - cell[:species, :])
            fresh = fresh - pair[0:species, pl.ds(at, LANES)]
            new[:, pl.ds(at, LANES)] = fresh
            weight = weights[pl.ds(b, 1), :]
            values = jnp.concatenate(
                [weight * fresh, weight, jnp.zeros((ROWS - species - 1, LANES), F32)], 0
            )
            top = values.astype(BF16)
            high[:, pl.ds(at, LANES)] = top
            low[:, pl.ds(at, LANES)] = (values - top.astype(F32)).astype(BF16)
            return 0

        lax.fori_loop(0, blocks, body, 0, unroll=4)
        acc1[...] = jnp.zeros(acc1.shape, F32)

        def scatter(k, _):
            rows = [slots[pl.ds(k * (per // LANES) + i, 1), :] for i in range(per // LANES)]
            group = (jnp.concatenate(rows, 1) >> 8) - there * (PLANE // 2)
            cols = pl.ds(pl.multiple_of(k * per, per), per)
            scatter_block(
                group, hot1[:, cols], high[:, cols], low[:, cols], left1, acc1, PLANE // 2
            )
            return 0

        lax.fori_loop(0, blocks * LANES // per, scatter, 0)
        for i in range(PLANE):
            moments[there * PLANE + i] = acc_row(acc1, i)

        def body_back(i, _):
            d = there * PLANE + lax.rem(inner + i, PLANE)
            copy_of(*back, me, d, d).start()
            return 0

        lax.fori_loop(first, PLANE, body_back, 0)

    far_first(lambda k: work(lax.rem(plane + planes - k, planes), 0))
    work(plane, 1)
    store = pltpu.make_async_copy(new, new_out, out_sem)
    store.start()
    returned[me] = moments[me]

    acc2[...] = jnp.zeros(acc2.shape, F32)

    def collect(there, first):
        wait_plane(back, there, first)
        at = [there * PLANE + i for i in range(PLANE)]
        values = jnp.concatenate([returned[s] for s in at], 1)
        index = jnp.concatenate([lists[pl.ds(s, 1), :] for s in at], 1)
        top = values.astype(BF16)
        rest = (values - top.astype(F32)).astype(BF16)
        scatter_block(index >> 8, hot_rows(index), top, rest, left2, acc2, count // 2)

    far_first(lambda k: collect(lax.rem(plane + k, planes), 0))
    collect(plane, 1)
    for j in range(count):
        total = acc_row(acc2, j)
        mean = (total[:species] + fields[j, 0:species, :]) / (total[species : species + 1] + 1.0)
        out[pl.ds(j, species, stride=count), :] = mean

    for i in range(4):

        @pl.when(sends[i])
        def _(i=i):
            halo_copy(i).wait_send()

    def finish(k, _):
        d = lax.rem(me + k, tiles)
        copy_of(*go, me, d, d).wait_send()
        copy_of(*back, me, d, d).wait_send()
        return 0

    lax.fori_loop(1, tiles, finish, 0)
    store.wait()


def hand_over(first, second, first_out, second_out):
    first_out[...] = first[...]
    second_out[...] = second[...]


def on_device(
    cell_means, diffusion, mix_rate, send_lists, compositions, weights, particle_slots, partners
):
    species, rows_x, rows_y, depth = cell_means.shape
    count = rows_x * rows_y
    tiles = send_lists.shape[1]
    particles = compositions.shape[1]
    blocks = particles // LANES
    vmem = lambda *shape: pltpu.VMEM(shape, F32)
    half_vmem = lambda *shape: pltpu.VMEM(shape, BF16)
    operands = (
        cell_means.reshape(species * count, depth),
        diffusion.reshape(count, depth),
        mix_rate.reshape(count, depth),
        send_lists[0],
        compositions,
        weights.reshape(blocks, LANES),
        particle_slots.reshape(blocks, LANES),
        partners.reshape(blocks, LANES),
    )
    out, new = pl.pallas_call(
        functools.partial(
            whole_kernel, lax.axis_size("gx"), lax.axis_size("gy"), rows_x, rows_y
        ),
        out_shape=(
            jax.ShapeDtypeStruct((species * count, LANES), F32),
            jax.ShapeDtypeStruct((species, particles), F32),
        ),
        in_specs=[pl.BlockSpec(memory_space=pltpu.HBM)] * 8,
        out_specs=[
            pl.BlockSpec(memory_space=pltpu.VMEM),
            pl.BlockSpec(memory_space=pltpu.HBM),
        ],
        name="whole_kernel",
        scratch_shapes=[pltpu.VMEM(a.shape, a.dtype) for a in operands]
        + [
            vmem(species, particles),
            vmem(rows_x, rows_y, ROWS, LANES),
            vmem(4, max(rows_x, rows_y), ROWS, LANES),
            vmem(count, ROWS, LANES),
            vmem(tiles, ROWS, LANES),
            vmem(tiles, ROWS, LANES),
            vmem(blocks, ROWS, LANES),
            vmem(tiles, ROWS, LANES),
            vmem(tiles, ROWS, LANES),
            half_vmem(particles // 256 * ROWS, 512),
            vmem(particles // 256 * ROWS, 256),
            vmem(ROWS, particles),
            half_vmem(ROWS, particles),
            half_vmem(ROWS, particles),
            half_vmem(256, particles),
            half_vmem(PLANE * ROWS, 1024),
            vmem(PLANE * ROWS, 256),
            half_vmem(count * ROWS, PLANE * LANES),
            vmem(count * ROWS, 256),
            pltpu.SemaphoreType.DMA((8,)),
            pltpu.SemaphoreType.DMA,
            pltpu.SemaphoreType.DMA((4,)),
            pltpu.SemaphoreType.DMA((4,)),
            pltpu.SemaphoreType.DMA((tiles,)),
            pltpu.SemaphoreType.DMA((tiles,)),
            pltpu.SemaphoreType.DMA((tiles,)),
            pltpu.SemaphoreType.DMA((tiles,)),
        ],
        compiler_params=pltpu.CompilerParams(
            collective_id=0, has_side_effects=True, vmem_limit_bytes=63 * 1024 * 1024
        ),
    )(*operands)
    out, new = pl.pallas_call(
        hand_over,
        out_shape=tuple(jax.ShapeDtypeStruct(a.shape, a.dtype) for a in (out, new)),
        in_specs=[pl.BlockSpec(memory_space=pltpu.VMEM)] * 2,
        out_specs=[pl.BlockSpec(memory_space=pltpu.VMEM)] * 2,
        name="hand_over",
    )(out, new)
    return out.reshape(species, rows_x, rows_y, depth), new


def solution(mesh):
    in_specs = (
        P(None, "gx", "gy", None),
        P("gx", "gy", None),
        P("gx", "gy", None),
        P(("gx", "gy"), None, None),
        P(None, ("gx", "gy")),
        P(("gx", "gy")),
        P(("gx", "gy")),
        P(("gx", "gy")),
    )
    out_specs = (P(None, "gx", "gy", None), P(None, ("gx", "gy")))
    return jax.shard_map(
        on_device, mesh=mesh, in_specs=in_specs, out_specs=out_specs, check_vma=False
    )
```

profile of v0, /device:TPU:0, one launch (start us, length us, event | category | flops | bytes accessed | tf_op | source)
XLA Modules:
  0.0 45.5 jit_solution(13292623344557346579)
XLA Ops:
  0.6 42.7 %whole_kernel.1 = (f32[480,128]{1,0:T(8,128)}, f32[30,4096]{1,0:T(8,128)}) custom-call(f32[480,128]{1,0:T(8,128)} %bitcast.8, f32[16,128]{1,0:T(8,128)} %bitcast.13, f32[16,128]{1,0:T(8,128)} %bitcast.14, s32[32,128]{1,0:T(8,128)} %bitcast.9, f32[30,4096]{1,0:T(8,128)} %refs_4_.1, f32[32,128]{1,0:T(8,128)} %bitcast.10, s32[32,128]{1,0:T(8,128)} %bitcast.11, ...), custom_call_target="tpu_custom_call" | custom-call | tf_op jit(solution)/shard_map/whole_kernel/pallas_call | solution.py:383
  43.4 2.1 %hand_over.1 = (f32[480,128]{1,0:T(8,128)}, f32[30,4096]{1,0:T(8,128)}) custom-call(f32[480,128]{1,0:T(8,128)} %get-tuple-element.6.first, f32[30,4096]{1,0:T(8,128)} %get-tuple-element.7.second), custom_call_target="tpu_custom_call" | custom-call | tf_op jit(solution)/shard_map/hand_over/pallas_call | solution.py:431
where the time goes:
time: 45.6 us; the launch traced here: 45.5 us
  Pallas kernels  44.8 us (98%)
  between operations  0.64 us (1%)
    pallas_call x1, Pallas kernels, on_device(): pl.pallas_call(functools.partial(whole_kernel, lax.axis_size('gx'), lax.a...  42.7 us
    pallas_call x1, Pallas kernels, on_device(): pl.pallas_call(hand_over, out_shape=tuple((jax.ShapeDtypeStruct(a.shape,...  2.07 us

commit v1 on v0

--- a/solution.py
+++ b/solution.py
@@ -117,16 +117,85 @@
     lax.fori_loop(0, particles // 256, body, 0)
 
 
+def pick_rates(lists, rates, buffer):
+    tiles = lists.shape[0]
+    for first in range(0, tiles, 8):
+        index = lists[first : first + 8, :]
+        lane, chunk = index & (LANES - 1), index >> 7
+        total = jnp.zeros((8, LANES), F32)
+        for j in range(rates.shape[0]):
+            row = jnp.broadcast_to(rates[j : j + 1, :], (8, LANES))
+            found = jnp.take_along_axis(row, lane, axis=1, mode="promise_in_bounds")
+            total = jnp.where(chunk == j, found, total)
+        for i in range(8):
+            buffer[first + i] = total[i : i + 1, :]
+
+
+def spread_rates(slots, rates, out):
+    blocks = slots.shape[0]
+    parts = range(0, blocks, 8)
+    lanes = [slots[b : b + 8, :] & (LANES - 1) for b in parts]
+    chunks = [slots[b : b + 8, :] >> 7 for b in parts]
+
+    def step(s, totals):
+        row = jnp.broadcast_to(rates[s], (8, LANES))
+        return tuple(
+            jnp.where(
+                chunk == s,
+                jnp.take_along_axis(row, lane, axis=1, mode="promise_in_bounds"),
+                total,
+            )
+            for lane, chunk, total in zip(lanes, chunks, totals)
+        )
+
+    start = tuple(jnp.zeros((8, LANES), F32) for _ in parts)
+    totals = lax.fori_loop(0, rates.shape[0], step, start, unroll=8)
+    for b, total in zip(parts, totals):
+        out[b : b + 8, :] = total
+
+
+def add_fields(received, slots, hot, table, parts, new):
+    species, particles = new.shape
+    groups = received.shape[0] // 2
+
+    def fill(h, _):
+        values = jnp.concatenate([received[2 * h], received[2 * h + 1]], 1)
+        first = values.astype(BF16)
+        at = pl.ds(pl.multiple_of(h * ROWS, ROWS), ROWS)
+        table[at, 0:256] = first
+        table[at, 256:512] = (values - first.astype(F32)).astype(BF16)
+        return 0
+
+    lax.fori_loop(0, groups, fill, 0)
+
+    def body(k, _):
+        at = pl.ds(pl.multiple_of(k * 256, 256), 256)
+        both = hot[:, at]
+        both = jnp.concatenate([both, both], 0)
+        parts[...] = jnp.dot(table[...], both, preferred_element_type=F32)
+        index = jnp.concatenate([slots[pl.ds(2 * k + i, 1), :] for i in range(2)], 1)
+        group = jnp.broadcast_to(index >> 8, (ROWS, 256))
+        total = jnp.zeros((ROWS, 256), F32)
+        for h in range(groups):
+            total = jnp.where(group == h, parts[h * ROWS : (h + 1) * ROWS, :], total)
+        new[:, at] += total[:species]
+        return 0
+
+    lax.fori_loop(0, particles // 256, body, 0)
+
+
 def whole_kernel(
     nx, ny, rows_x, rows_y, *refs
 ):
-    inputs, (out, new_out), refs = refs[:8], refs[8:10], refs[10:]
+    inputs, (out, new), refs = refs[:8], refs[8:10], refs[10:]
     staged, refs = refs[:8], refs[8:]
     means, diffusion, rate, lists, compositions, weights, slots, partners = staged
     (
-        new, cells, halo, fields, outgoing, received, local, moments, returned,
-        table, parts, pair, high, low, hot1, left1, acc1, left2, acc2,
-        in_sems, out_sem, halo_send, halo_recv, go_send, go_recv, back_send, back_recv,
+        cells, halo, fields, scaled, rates_out, rates_in, rates, outgoing, received, moments,
+        returned, table, parts, pair, high, low, hot1, left1, acc1, field_table, field_parts,
+        left2, acc2,
+        in_sems, halo_send, halo_recv, rate_send, rate_recv, go_send, go_recv,
+        back_send, back_recv,
     ) = refs
     tiles = nx * ny
     planes = tiles // PLANE
@@ -143,7 +212,7 @@
     loads = [
         pltpu.make_async_copy(inputs[i], staged[i], in_sems.at[i]) for i in range(8)
     ]
-    for i in (0, 1, 2, 4, 7, 3, 6, 5):
+    for i in (2, 3, 0, 1, 6, 4, 7, 5):
         loads[i].start()
 
     barrier = pltpu.get_barrier_semaphore()
@@ -157,12 +226,17 @@
 
     lax.fori_loop(1, tiles, greet, 0)
 
+    loads[2].wait()
+    loads[3].wait()
+    blend = 1.0 - jnp.exp(-rate[...])
+    pick_rates(lists, blend, rates_out)
     loads[0].wait()
     for x in range(rows_x):
         for y in range(rows_y):
             j = x * rows_y + y
             cells[x, y, 0:species, :] = means[pl.ds(j, species, stride=count), :]
             cells[x, y, species:ROWS, :] = jnp.zeros((ROWS - species, LANES), F32)
+    rates_in[me] = rates_out[me]
 
     pl.semaphore_wait(barrier, tiles - 1)
 
@@ -194,15 +268,28 @@
         def _(i=i):
             halo[i] = jnp.zeros(halo.shape[1:], F32)
 
-    loads[4].wait()
-    loads[7].wait()
-    gather_pairs(compositions, partners, table, parts, pair)
-    for i in (1, 2, 3, 5, 6):
-        loads[i].wait()
+    def rate_copy(source, d, target):
+        return pltpu.make_async_remote_copy(
+            src_ref=rates_out.at[d],
+            dst_ref=rates_in.at[source],
+            send_sem=rate_send.at[d],
+            recv_sem=rate_recv.at[source],
+            device_id=place(target),
+            device_id_type=pl.DeviceIdType.MESH,
+        )
+
+    def send_rates(k, _):
+        d = lax.rem(me + k, tiles)
+        rate_copy(me, d, d).start()
+        return 0
+
+    lax.fori_loop(1, tiles, send_rates, 0)
+
+    loads[6].wait()
     for b in range(0, blocks, 4):
         index = jnp.concatenate([slots[b + i : b + i + 1, :] for i in range(4)], 1)
         hot1[:, b * LANES : (b + 4) * LANES] = hot_rows(index)
-    local[...] = jnp.zeros(local.shape, F32)
+    loads[1].wait()
 
     for i in range(4):
 
@@ -211,25 +298,25 @@
             halo_copy(i).wait_recv()
 
     stencil(cells, halo, diffusion, fields, rows_x, rows_y)
-    blend = 1.0 - jnp.exp(-rate[...])
-    for j in range(count):
-        fields[j, species : species + 1, :] = blend[j : j + 1, :]
-
-    def copy_of(buffers, sems, source, d, target):
+
+    def copy_of(buffers, sems, rows, source, d, target):
         return pltpu.make_async_remote_copy(
-            src_ref=buffers[0].at[d, 0 : species + 1],
-            dst_ref=buffers[1].at[source, 0 : species + 1],
+            src_ref=buffers[0].at[d, 0:rows],
+            dst_ref=buffers[1].at[source, 0:rows],
             send_sem=sems[0].at[d],
             recv_sem=sems[1].at[source],
             device_id=place(target),
             device_id_type=pl.DeviceIdType.MESH,
         )
 
-    go = (outgoing, received), (go_send, go_recv)
-    back = (moments, returned), (back_send, back_recv)
+    go = (outgoing, received), (go_send, go_recv), species
+    back = (moments, returned), (back_send, back_recv), species + 1
+
+    for j in range(count):
+        scaled[j] = fields[j] * blend[j : j + 1, :]
 
     def fill(d, buffer, row):
-        found = pick(fields, count, lists[pl.ds(d, 1), :])
+        found = pick(scaled, count, lists[pl.ds(d, 1), :])
         for g in range(GROUPS):
             buffer[row, 8 * g : 8 * g + 8, :] = found[g]
 
@@ -251,80 +338,89 @@
     fill(me, received, me)
     send_plane(plane, 1)
 
-    def wait_plane(which, there, first):
+    loads[4].wait()
+    loads[7].wait()
+    gather_pairs(compositions, partners, table, parts, pair)
+    loads[5].wait()
+
+    def wait_rates(k, _):
+        s = lax.rem(me + k, tiles)
+        rate_copy(s, s, s).wait_recv()
+        return 0
+
+    lax.fori_loop(1, tiles, wait_rates, 0)
+    spread_rates(slots, rates_in, rates)
+
+    def weigh(b, _):
+        at = pl.ds(pl.multiple_of(b * LANES, LANES), LANES)
+        mine = compositions[:, at]
+        fresh = mine - rates[pl.ds(b, 1), :] * mine - pair[0:species, at]
+        new[:, at] = fresh
+        weight = weights[pl.ds(b, 1), :]
+        values = jnp.concatenate(
+            [weight * fresh, weight, jnp.zeros((ROWS - species - 1, LANES), F32)], 0
+        )
+        top = values.astype(BF16)
+        high[:, at] = top
+        low[:, at] = (values - top.astype(F32)).astype(BF16)
+        return 0
+
+    lax.fori_loop(0, blocks, weigh, 0, unroll=4)
+
+    per = left1.shape[1]
+    wide = acc1.shape[0] // ROWS
+
+    def sum_slots(part, last):
+        acc1[...] = jnp.zeros(acc1.shape, F32)
+
+        def scatter(k, _):
+            rows = [slots[pl.ds(k * (per // LANES) + i, 1), :] for i in range(per // LANES)]
+            group = (jnp.concatenate(rows, 1) >> 8) - part * (wide // 2)
+            cols = pl.ds(pl.multiple_of(k * per, per), per)
+            scatter_block(
+                group, hot1[:, cols], high[:, cols], low[:, cols], left1, acc1, wide // 2
+            )
+            return 0
+
+        lax.fori_loop(0, blocks * LANES // per, scatter, 0)
+        for i in range(wide):
+            moments[part * wide + i] = acc_row(acc1, i)
+        inside = lax.rem(me, wide)
+
+        def body(i, _):
+            d = part * wide + lax.rem(inside + i, wide)
+            copy_of(*back, me, d, d).start()
+            return 0
+
+        lax.fori_loop(last, wide, body, 0)
+
+    own = lax.div(me, wide)
+
+    def other(k, _):
+        sum_slots(lax.rem(own + k, tiles // wide), 0)
+        return 0
+
+    lax.fori_loop(1, tiles // wide, other, 0)
+    sum_slots(own, 1)
+    returned[me] = moments[me]
+
+    def wait_go(k, _):
+        s = lax.rem(me + k, tiles)
+        copy_of(*go, s, s, s).wait_recv()
+        return 0
+
+    lax.fori_loop(1, tiles, wait_go, 0)
+    add_fields(received, slots, hot1, field_table, field_parts, new)
+
+    acc2[...] = jnp.zeros(acc2.shape, F32)
+
+    def collect(there, first):
         def body(i, _):
             s = there * PLANE + lax.rem(inner + i, PLANE)
-            copy_of(*which, s, s, s).wait_recv()
+            copy_of(*back, s, s, s).wait_recv()
             return 0
 
         lax.fori_loop(first, PLANE, body, 0)
-
-    per = left1.shape[1]
-
-    def work(there, first):
-        wait_plane(go, there, first)
-
-        def body(b, _):
-            index = slots[pl.ds(b, 1), :]
-            lane = jnp.broadcast_to(index & (LANES - 1), (8, LANES))
-            chunk = jnp.broadcast_to((index >> 7) - there * PLANE, (8, LANES))
-            sums = [local[b, 8 * g : 8 * g + 8, :] for g in range(GROUPS)]
-            for i in range(PLANE):
-                mask = chunk == i
-                for g in range(GROUPS):
-                    rows = received[there * PLANE + i, 8 * g : 8 * g + 8, :]
-                    found = jnp.take_along_axis(rows, lane, axis=1, mode="promise_in_bounds")
-                    sums[g] = jnp.where(mask, found, sums[g])
-            for g in range(GROUPS):
-                local[b, 8 * g : 8 * g + 8, :] = sums[g]
-            at = pl.multiple_of(b * LANES, LANES)
-            cell = jnp.concatenate(sums, 0)
-            mine = compositions[:, pl.ds(at, LANES)]
-            fresh = mine - cell[species : species + 1, :] * (mine - cell[:species, :])
-            fresh = fresh - pair[0:species, pl.ds(at, LANES)]
-            new[:, pl.ds(at, LANES)] = fresh
-            weight = weights[pl.ds(b, 1), :]
-            values = jnp.concatenate(
-                [weight * fresh, weight, jnp.zeros((ROWS - species - 1, LANES), F32)], 0
-            )
-            top = values.astype(BF16)
-            high[:, pl.ds(at, LANES)] = top
-            low[:, pl.ds(at, LANES)] = (values - top.astype(F32)).astype(BF16)
-            return 0
-
-        lax.fori_loop(0, blocks, body, 0, unroll=4)
-        acc1[...] = jnp.zeros(acc1.shape, F32)
-
-        def scatter(k, _):
-            rows = [slots[pl.ds(k * (per // LANES) + i, 1), :] for i in range(per // LANES)]
-            group = (jnp.concatenate(rows, 1) >> 8) - there * (PLANE // 2)
-            cols = pl.ds(pl.multiple_of(k * per, per), per)
-            scatter_block(
-                group, hot1[:, cols], high[:, cols], low[:, cols], left1, acc1, PLANE // 2
-            )
-            return 0
-
-        lax.fori_loop(0, blocks * LANES // per, scatter, 0)
-        for i in range(PLANE):
-            moments[there * PLANE + i] = acc_row(acc1, i)
-
-        def body_back(i, _):
-            d = there * PLANE + lax.rem(inner + i, PLANE)
-            copy_of(*back, me, d, d).start()
-            return 0
-
-        lax.fori_loop(first, PLANE, body_back, 0)
-
-    far_first(lambda k: work(lax.rem(plane + planes - k, planes), 0))
-    work(plane, 1)
-    store = pltpu.make_async_copy(new, new_out, out_sem)
-    store.start()
-    returned[me] = moments[me]
-
-    acc2[...] = jnp.zeros(acc2.shape, F32)
-
-    def collect(there, first):
-        wait_plane(back, there, first)
         at = [there * PLANE + i for i in range(PLANE)]
         values = jnp.concatenate([returned[s] for s in at], 1)
         index = jnp.concatenate([lists[pl.ds(s, 1), :] for s in at], 1)
@@ -332,11 +428,15 @@
         rest = (values - top.astype(F32)).astype(BF16)
         scatter_block(index >> 8, hot_rows(index), top, rest, left2, acc2, count // 2)
 
-    far_first(lambda k: collect(lax.rem(plane + k, planes), 0))
     collect(plane, 1)
+    lax.fori_loop(
+        1, planes, lambda k, _: (collect(lax.rem(plane + k, planes), 0), 0)[1], 0
+    )
     for j in range(count):
         total = acc_row(acc2, j)
-        mean = (total[:species] + fields[j, 0:species, :]) / (total[species : species + 1] + 1.0)
+        weight = total[species : species + 1]
+        mixed = scaled[j, 0:species, :] * weight
+        mean = (total[:species] + mixed + fields[j, 0:species, :]) / (weight + 1.0)
         out[pl.ds(j, species, stride=count), :] = mean
 
     for i in range(4):
@@ -347,17 +447,23 @@
 
     def finish(k, _):
         d = lax.rem(me + k, tiles)
+        rate_copy(me, d, d).wait_send()
         copy_of(*go, me, d, d).wait_send()
         copy_of(*back, me, d, d).wait_send()
         return 0
 
     lax.fori_loop(1, tiles, finish, 0)
-    store.wait()
-
-
-def hand_over(first, second, first_out, second_out):
-    first_out[...] = first[...]
-    second_out[...] = second[...]
+
+
+def hand_over(first, second, first_out, second_out, sems):
+    copies = [
+        pltpu.make_async_copy(first, first_out, sems.at[0]),
+        pltpu.make_async_copy(second, second_out, sems.at[1]),
+    ]
+    for copy in copies:
+        copy.start()
+    for copy in copies:
+        copy.wait()
 
 
 def on_device(
@@ -385,24 +491,23 @@
             whole_kernel, lax.axis_size("gx"), lax.axis_size("gy"), rows_x, rows_y
         ),
         out_shape=(
-            jax.ShapeDtypeStruct((species * count, LANES), F32),
-            jax.ShapeDtypeStruct((species, particles), F32),
+            pltpu.VMEM((species * count, LANES), F32),
+            pltpu.VMEM((species, particles), F32),
         ),
         in_specs=[pl.BlockSpec(memory_space=pltpu.HBM)] * 8,
-        out_specs=[
-            pl.BlockSpec(memory_space=pltpu.VMEM),
-            pl.BlockSpec(memory_space=pltpu.HBM),
-        ],
+        out_specs=[pl.BlockSpec(memory_space=pltpu.VMEM)] * 2,
         name="whole_kernel",
         scratch_shapes=[pltpu.VMEM(a.shape, a.dtype) for a in operands]
         + [
-            vmem(species, particles),
             vmem(rows_x, rows_y, ROWS, LANES),
             vmem(4, max(rows_x, rows_y), ROWS, LANES),
             vmem(count, ROWS, LANES),
+            vmem(count, ROWS, LANES),
+            vmem(tiles, 1, LANES),
+            vmem(tiles, 1, LANES),
+            vmem(blocks, LANES),
             vmem(tiles, ROWS, LANES),
             vmem(tiles, ROWS, LANES),
-            vmem(blocks, ROWS, LANES),
             vmem(tiles, ROWS, LANES),
             vmem(tiles, ROWS, LANES),
             half_vmem(particles // 256 * ROWS, 512),
@@ -411,14 +516,17 @@
             half_vmem(ROWS, particles),
             half_vmem(ROWS, particles),
             half_vmem(256, particles),
-            half_vmem(PLANE * ROWS, 1024),
-            vmem(PLANE * ROWS, 256),
+            half_vmem(2 * PLANE * ROWS, 1024),
+            vmem(2 * PLANE * ROWS, 256),
+            half_vmem(tiles // 2 * ROWS, 512),
+            vmem(tiles // 2 * ROWS, 256),
             half_vmem(count * ROWS, PLANE * LANES),
             vmem(count * ROWS, 256),
             pltpu.SemaphoreType.DMA((8,)),
-            pltpu.SemaphoreType.DMA,
             pltpu.SemaphoreType.DMA((4,)),
             pltpu.SemaphoreType.DMA((4,)),
+            pltpu.SemaphoreType.DMA((tiles,)),
+            pltpu.SemaphoreType.DMA((tiles,)),
             pltpu.SemaphoreType.DMA((tiles,)),
             pltpu.SemaphoreType.DMA((tiles,)),
             pltpu.SemaphoreType.DMA((tiles,)),
@@ -432,7 +540,9 @@
         hand_over,
         out_shape=tuple(jax.ShapeDtypeStruct(a.shape, a.dtype) for a in (out, new)),
         in_specs=[pl.BlockSpec(memory_space=pltpu.VMEM)] * 2,
-        out_specs=[pl.BlockSpec(memory_space=pltpu.VMEM)] * 2,
+        out_specs=[pl.BlockSpec(memory_space=pltpu.HBM)] * 2,
+        scratch_shapes=[pltpu.SemaphoreType.DMA((2,))],
+        compiler_params=pltpu.CompilerParams(vmem_limit_bytes=1024 * 1024),
         name="hand_over",
     )(out, new)
     return out.reshape(species, rows_x, rows_y, depth), new

time: 45.6 us -> 41.6 us (0.912)
  Pallas kernels: 44.8 us -> 40.7 us
    pallas_call x1, Pallas kernels: 42.7 us -> 39.8 us  [on_device(): pl.pallas_call(functools.partial(whole_kernel, lax.axis_size('gx'), lax.a...]
    pallas_call x1, Pallas kernels: 2.07 us -> 0.89 us  [on_device(): pl.pallas_call(hand_over, out_shape=tuple((jax.ShapeDtypeStruct(a.shape,...]
where the time goes in v1:
time: 41.6 us; the launch traced here: 41.4 us
  Pallas kernels  40.7 us (98%)
  between operations  0.64 us (2%)
    pallas_call x1, Pallas kernels, on_device(): pl.pallas_call(functools.partial(whole_kernel, lax.axis_size('gx'), lax.a...  39.8 us
    pallas_call x1, Pallas kernels, on_device(): pl.pallas_call(hand_over, out_shape=tuple((jax.ShapeDtypeStruct(a.shape,...  0.89 us

profile of v1, /device:TPU:0, one launch (start us, length us, event | category | flops | bytes accessed | tf_op | source)
XLA Modules:
  0.0 41.4 jit_solution(6441303793293532178)
XLA Ops:
  0.6 39.8 %whole_kernel.1 = (f32[480,128]{1,0:T(8,128)S(1)}, f32[30,4096]{1,0:T(8,128)S(1)}) custom-call(f32[480,128]{1,0:T(8,128)} %bitcast.8, f32[16,128]{1,0:T(8,128)} %bitcast.13, f32[16,128]{1,0:T(8,128)} %bitcast.14, s32[32,128]{1,0:T(8,128)} %bitcast.9, f32[30,4096]{1,0:T(8,128)} %refs_4_.1, f32[32,128]{1,0:T(8,128)} %bitcast.10, s32[32,128]{1,0:T(8,128)} %bitcast.11, ...), custom_call_target="tpu_custom_call" | custom-call | tf_op jit(solution)/shard_map/whole_kernel/pallas_call | solution.py:489
  40.5 0.9 %hand_over.1 = (f32[480,128]{1,0:T(8,128)}, f32[30,4096]{1,0:T(8,128)}) custom-call(f32[480,128]{1,0:T(8,128)S(1)} %get-tuple-element.6.first, f32[30,4096]{1,0:T(8,128)S(1)} %get-tuple-element.7.second), custom_call_target="tpu_custom_call" | custom-call | tf_op jit(solution)/shard_map/hand_over/pallas_call | solution.py:539

commit v2 on v1

--- a/solution.py
+++ b/solution.py
@@ -12,33 +12,27 @@
 ROWS = 32
 GROUPS = ROWS // 8
 PLANE = 8
+WIDE = 1024
+FIRST = 0
+HALO_ROUNDS = 2
 F32 = jnp.float32
 BF16 = jnp.bfloat16
 
 
-def pick(table, count, index, start=0, sums=None):
-    lane = jnp.broadcast_to(index & (LANES - 1), (8, LANES))
-    chunk = jnp.broadcast_to(index >> 7, (8, LANES))
-    if sums is None:
-        sums = tuple(jnp.zeros((8, LANES), F32) for _ in range(GROUPS))
-
-    def step(at, sums):
-        mask = chunk == at
-        return tuple(
-            jnp.where(
-                mask,
-                jnp.take_along_axis(
-                    table[at, 8 * g : 8 * g + 8, :], lane, axis=1, mode="promise_in_bounds"
-                ),
-                total,
-            )
-            for g, total in enumerate(sums)
-        )
-
-    return lax.fori_loop(start, start + count, step, sums, unroll=min(count, 16))
-
-
-def stencil(cells, halo, diffusion, fields, rows_x, rows_y):
+def select_group(index, parts, groups):
+    group = jnp.broadcast_to(index >> 8, (ROWS, index.shape[1]))
+    total = jnp.zeros(group.shape, F32)
+    for h in range(groups):
+        total = jnp.where(group == h, parts[h * ROWS : (h + 1) * ROWS, :], total)
+    return total
+
+
+def row_block(table, k, width):
+    many = width // LANES
+    return jnp.concatenate([table[pl.ds(k * many + i, 1), :] for i in range(many)], 1)
+
+
+def stencil(cells, halo, diffusion, fields, blend, scaled, table, rows_x, rows_y):
     lane = lax.broadcasted_iota(jnp.int32, (ROWS, LANES), 1)
     for x in range(rows_x):
         for y in range(rows_y):
@@ -50,7 +44,15 @@
             total = total + jnp.where(lane < LANES - 1, pltpu.roll(mid, LANES - 1, 1), 0.0)
             total = total + jnp.where(lane > 0, pltpu.roll(mid, 1, 1), 0.0)
             j = x * rows_y + y
-            fields[j] = mid + diffusion[j : j + 1, :] * (total - 6.0 * mid)
+            filtered = mid + diffusion[j : j + 1, :] * (total - 6.0 * mid)
+            fields[j] = filtered
+            mixed = filtered * blend[j : j + 1, :]
+            scaled[j] = mixed
+            first = mixed.astype(BF16)
+            rows = slice(j // 2 * ROWS, (j // 2 + 1) * ROWS)
+            at = j % 2 * LANES
+            table[rows, at : at + LANES] = first
+            table[rows, 256 + at : 256 + at + LANES] = (mixed - first.astype(F32)).astype(BF16)
 
 
 def scatter_block(group, hot, high, low, left, acc, groups):
@@ -88,33 +90,31 @@
             cells[x, y, species:ROWS, :] = jnp.zeros((ROWS - species, LANES), F32)
 
 
-def gather_pairs(compositions, partners, table, parts, pair):
+def split_table(compositions, table):
     species, particles = compositions.shape
-    groups = particles // 256
-    for h in range(groups):
+    for h in range(particles // 256):
         values = compositions[:, h * 256 : (h + 1) * 256]
         values = jnp.concatenate([values, jnp.zeros((ROWS - species, 256), F32)], 0)
         first = values.astype(BF16)
         table[h * ROWS : (h + 1) * ROWS, 0:256] = first
         table[h * ROWS : (h + 1) * ROWS, 256:512] = (values - first.astype(F32)).astype(BF16)
 
+
+def gather_pairs(compositions, partners, table, parts, pair, first, last):
+    species, particles = compositions.shape
+
     def body(k, _):
-        index = jnp.concatenate([partners[pl.ds(2 * k + i, 1), :] for i in range(2)], 1)
-        place = lax.broadcasted_iota(jnp.int32, (256, 256), 0)
-        hot = jnp.where(place == (index & 255), 1.0, 0.0).astype(BF16)
-        hot = jnp.concatenate([hot, hot], 0)
-        parts[...] = jnp.dot(table[...], hot, preferred_element_type=F32)
-        group = jnp.broadcast_to(index >> 8, (ROWS, 256))
-        total = jnp.zeros((ROWS, 256), F32)
-        for h in range(groups):
-            total = jnp.where(group == h, parts[h * ROWS : (h + 1) * ROWS, :], total)
-        at = pl.multiple_of(k * 256, 256)
-        pair[0:species, pl.ds(at, 256)] = PAIR_RATE * (
-            compositions[:, pl.ds(at, 256)] - total[:species]
-        )
-        return 0
-
-    lax.fori_loop(0, particles // 256, body, 0)
+        index = row_block(partners, k, WIDE)
+        hot = hot_rows(index)
+        parts[...] = jnp.dot(
+            table[...], jnp.concatenate([hot, hot], 0), preferred_element_type=F32
+        )
+        total = select_group(index, parts, particles // 256)
+        at = pl.ds(pl.multiple_of(k * WIDE, WIDE), WIDE)
+        pair[0:species, at] = PAIR_RATE * (compositions[:, at] - total[:species])
+        return 0
+
+    lax.fori_loop(first, last, body, 0)
 
 
 def pick_rates(lists, rates, buffer):
@@ -156,32 +156,30 @@
 
 def add_fields(received, slots, hot, table, parts, new):
     species, particles = new.shape
-    groups = received.shape[0] // 2
-
-    def fill(h, _):
-        values = jnp.concatenate([received[2 * h], received[2 * h + 1]], 1)
-        first = values.astype(BF16)
-        at = pl.ds(pl.multiple_of(h * ROWS, ROWS), ROWS)
-        table[at, 0:256] = first
-        table[at, 256:512] = (values - first.astype(F32)).astype(BF16)
-        return 0
-
-    lax.fori_loop(0, groups, fill, 0)
-
-    def body(k, _):
-        at = pl.ds(pl.multiple_of(k * 256, 256), 256)
-        both = hot[:, at]
-        both = jnp.concatenate([both, both], 0)
-        parts[...] = jnp.dot(table[...], both, preferred_element_type=F32)
-        index = jnp.concatenate([slots[pl.ds(2 * k + i, 1), :] for i in range(2)], 1)
-        group = jnp.broadcast_to(index >> 8, (ROWS, 256))
-        total = jnp.zeros((ROWS, 256), F32)
+    groups = table.shape[0] // ROWS
+
+    def chunk(c, _):
         for h in range(groups):
-            total = jnp.where(group == h, parts[h * ROWS : (h + 1) * ROWS, :], total)
-        new[:, at] += total[:species]
-        return 0
-
-    lax.fori_loop(0, particles // 256, body, 0)
+            s = 2 * (c * groups + h)
+            values = jnp.concatenate([received[s], received[s + 1]], 1)
+            first = values.astype(BF16)
+            rows = slice(h * ROWS, (h + 1) * ROWS)
+            table[rows, 0:256] = first
+            table[rows, 256:512] = (values - first.astype(F32)).astype(BF16)
+
+        def body(k, _):
+            at = pl.ds(pl.multiple_of(k * WIDE, WIDE), WIDE)
+            both = hot[:, at]
+            parts[...] = jnp.dot(
+                table[...], jnp.concatenate([both, both], 0), preferred_element_type=F32
+            )
+            index = row_block(slots, k, WIDE) - c * (groups * 256)
+            new[:, at] += select_group(index, parts, groups)[:species]
+            return 0
+
+        return lax.fori_loop(0, particles // WIDE, body, 0)
+
+    lax.fori_loop(0, received.shape[0] // 2 // groups, chunk, 0)
 
 
 def whole_kernel(
@@ -192,10 +190,9 @@
     means, diffusion, rate, lists, compositions, weights, slots, partners = staged
     (
         cells, halo, fields, scaled, rates_out, rates_in, rates, outgoing, received, moments,
-        returned, table, parts, pair, high, low, hot1, left1, acc1, field_table, field_parts,
-        left2, acc2,
+        returned, table, parts, pair, high, low, hot1, hot2, left1, acc1, field_table, left2, acc2,
         in_sems, halo_send, halo_recv, rate_send, rate_recv, go_send, go_recv,
-        back_send, back_recv,
+        back_send, back_recv, late,
     ) = refs
     tiles = nx * ny
     planes = tiles // PLANE
@@ -212,44 +209,67 @@
     loads = [
         pltpu.make_async_copy(inputs[i], staged[i], in_sems.at[i]) for i in range(8)
     ]
-    for i in (2, 3, 0, 1, 6, 4, 7, 5):
+    for i in (0, 4, 7, 2, 3, 6, 1, 5):
         loads[i].start()
 
     barrier = pltpu.get_barrier_semaphore()
 
-    def greet(k, _):
-        d = lax.rem(me + k, tiles)
+    def signal(semaphore, d):
         pl.semaphore_signal(
-            barrier, inc=1, device_id=place(d), device_id_type=pl.DeviceIdType.MESH
-        )
-        return 0
-
-    lax.fori_loop(1, tiles, greet, 0)
-
-    loads[2].wait()
-    loads[3].wait()
-    blend = 1.0 - jnp.exp(-rate[...])
-    pick_rates(lists, blend, rates_out)
+            semaphore, inc=1, device_id=place(d), device_id_type=pl.DeviceIdType.MESH
+        )
+
+    def greet_plane(k, _):
+        signal(barrier, plane * PLANE + lax.rem(inner + k, PLANE))
+        return 0
+
+    def greet(d, _):
+        signal(barrier, d)
+        return 0
+
+    def announce(d, _):
+        signal(late, d)
+        return 0
+
+    lax.fori_loop(1, PLANE, greet_plane, 0)
+    above = jnp.logical_and(gx < nx - 1, lax.div(me + ny, PLANE) > plane)
+    below = jnp.logical_and(gx > 0, lax.div(me - ny + tiles, PLANE) < plane + planes)
+
+    @pl.when(below)
+    def _():
+        signal(barrier, me - ny)
+
+    lax.fori_loop((plane + 1) * PLANE, tiles, greet, 0)
+
     loads[0].wait()
     for x in range(rows_x):
         for y in range(rows_y):
             j = x * rows_y + y
             cells[x, y, 0:species, :] = means[pl.ds(j, species, stride=count), :]
             cells[x, y, species:ROWS, :] = jnp.zeros((ROWS - species, LANES), F32)
-    rates_in[me] = rates_out[me]
-
-    pl.semaphore_wait(barrier, tiles - 1)
+
+    rounds = blocks * LANES // WIDE
+    hops = lax.div(gx, 2) + lax.rem(gx, 2) + lax.div(gy, 2)
+    early = jnp.where(hops == 0, FIRST, 0)
+    early = jnp.minimum(early, rounds)
+    soon = jnp.minimum(early + HALO_ROUNDS, rounds)
+    loads[4].wait()
+    loads[7].wait()
+    split_table(compositions, table)
+    gather_pairs(compositions, partners, table, parts, pair, 0, early)
+
+    pl.semaphore_wait(barrier, (plane + 1) * PLANE - 1 + above.astype(jnp.int32))
 
     def halo_copy(i):
         source, length, target = (
-            (cells.at[rows_x - 1], rows_y, (gx + 1, gy)),
-            (cells.at[0], rows_y, (gx - 1, gy)),
-            (cells.at[:, rows_y - 1], rows_x, (gx, gy + 1)),
-            (cells.at[:, 0], rows_x, (gx, gy - 1)),
+            (cells.at[rows_x - 1, :, 0:species], rows_y, (gx + 1, gy)),
+            (cells.at[0, :, 0:species], rows_y, (gx - 1, gy)),
+            (cells.at[:, rows_y - 1, 0:species], rows_x, (gx, gy + 1)),
+            (cells.at[:, 0, 0:species], rows_x, (gx, gy - 1)),
         )[i]
         return pltpu.make_async_remote_copy(
             src_ref=source,
-            dst_ref=halo.at[i, 0:length],
+            dst_ref=halo.at[i, 0:length, 0:species],
             send_sem=halo_send.at[i],
             recv_sem=halo_recv.at[i],
             device_id=target,
@@ -264,9 +284,19 @@
         def _(i=i):
             halo_copy(i).start()
 
+    lax.fori_loop(0, plane * PLANE, announce, 0)
+    for i in range(4):
+        halo[i, :, species:ROWS] = jnp.zeros(halo[i, :, species:ROWS].shape, F32)
+
         @pl.when(jnp.logical_not(receives[i]))
         def _(i=i):
-            halo[i] = jnp.zeros(halo.shape[1:], F32)
+            halo[i, :, 0:species] = jnp.zeros(halo[i, :, 0:species].shape, F32)
+
+    loads[2].wait()
+    loads[3].wait()
+    blend = 1.0 - jnp.exp(-rate[...])
+    pick_rates(lists, blend, rates_out)
+    rates_in[me] = rates_out[me]
 
     def rate_copy(source, d, target):
         return pltpu.make_async_remote_copy(
@@ -283,13 +313,73 @@
         rate_copy(me, d, d).start()
         return 0
 
-    lax.fori_loop(1, tiles, send_rates, 0)
 
     loads[6].wait()
     for b in range(0, blocks, 4):
-        index = jnp.concatenate([slots[b + i : b + i + 1, :] for i in range(4)], 1)
-        hot1[:, b * LANES : (b + 4) * LANES] = hot_rows(index)
+        hot1[:, b * LANES : (b + 4) * LANES] = hot_rows(row_block(slots, b // 4, 4 * LANES))
+    for b in range(0, tiles, 4):
+        hot2[:, b * LANES : (b + 4) * LANES] = hot_rows(row_block(lists, b // 4, 4 * LANES))
     loads[1].wait()
+    gather_pairs(compositions, partners, table, parts, pair, early, soon)
+
+    @pl.when(plane < planes - 1)
+    def _():
+        pl.semaphore_wait(late, tiles - (plane + 1) * PLANE)
+
+    lax.fori_loop(1, tiles, send_rates, 0)
+
+    def go_copy(source, d, target):
+        return pltpu.make_async_remote_copy(
+            src_ref=outgoing.at[d, 0:species],
+            dst_ref=received.at[source, 0:species],
+            send_sem=go_send.at[d],
+            recv_sem=go_recv.at[source],
+            device_id=place(target),
+            device_id_type=pl.DeviceIdType.MESH,
+        )
+
+    def back_copy(source, d, target):
+        return pltpu.make_async_remote_copy(
+            src_ref=moments.at[d, 0 : species + 1],
+            dst_ref=returned.at[source, 0 : species + 1],
+            send_sem=back_send.at[d],
+            recv_sem=back_recv.at[source],
+            device_id=place(target),
+            device_id_type=pl.DeviceIdType.MESH,
+        )
+
+    wide = acc1.shape[0] // ROWS
+    sections = tiles // wide
+    own = lax.div(me, wide)
+    per_section = wide // PLANE
+
+    def peer(section, k):
+        turn = lax.div(k, PLANE)
+        near = lax.rem(plane + 1 + turn, per_section)
+        turn = jnp.where(section == own, near, turn)
+        return section * wide + turn * PLANE + lax.rem(inner + k, PLANE)
+
+    def fill(there):
+        at = pl.ds(pl.multiple_of(there * (PLANE * LANES), PLANE * LANES), PLANE * LANES)
+        hot = hot2[:, at]
+        parts[0 : count // 2 * ROWS, :] = jnp.dot(
+            field_table[...], jnp.concatenate([hot, hot], 0), preferred_element_type=F32
+        )
+        index = row_block(lists, there, PLANE * LANES)
+        found = select_group(index, parts, count // 2)
+        for i in range(PLANE):
+            outgoing[there * PLANE + i] = found[:, i * LANES : (i + 1) * LANES]
+
+    def send_go(there, first):
+        def body(k, _):
+            d = there * PLANE + lax.rem(inner + k, PLANE)
+            go_copy(me, d, d).start()
+            return 0
+
+        lax.fori_loop(first, PLANE, body, 0)
+
+    def far_plane(k):
+        return lax.rem(own * per_section + k, planes)
 
     for i in range(4):
 
@@ -297,50 +387,17 @@
         def _(i=i):
             halo_copy(i).wait_recv()
 
-    stencil(cells, halo, diffusion, fields, rows_x, rows_y)
-
-    def copy_of(buffers, sems, rows, source, d, target):
-        return pltpu.make_async_remote_copy(
-            src_ref=buffers[0].at[d, 0:rows],
-            dst_ref=buffers[1].at[source, 0:rows],
-            send_sem=sems[0].at[d],
-            recv_sem=sems[1].at[source],
-            device_id=place(target),
-            device_id_type=pl.DeviceIdType.MESH,
-        )
-
-    go = (outgoing, received), (go_send, go_recv), species
-    back = (moments, returned), (back_send, back_recv), species + 1
-
-    for j in range(count):
-        scaled[j] = fields[j] * blend[j : j + 1, :]
-
-    def fill(d, buffer, row):
-        found = pick(scaled, count, lists[pl.ds(d, 1), :])
-        for g in range(GROUPS):
-            buffer[row, 8 * g : 8 * g + 8, :] = found[g]
-
-    def send_plane(there, first):
-        def body(i, _):
-            d = there * PLANE + lax.rem(inner + i, PLANE)
-            fill(d, outgoing, d)
-            copy_of(*go, me, d, d).start()
-            return 0
-
-        lax.fori_loop(first, PLANE, body, 0)
-
-    def far_first(step):
-        half = planes // 2
-        lax.fori_loop(half, planes, lambda k, _: (step(k), 0)[1], 0)
-        lax.fori_loop(1, half, lambda k, _: (step(half - k), 0)[1], 0)
-
-    far_first(lambda k: send_plane(lax.rem(plane + k, planes), 0))
-    fill(me, received, me)
-    send_plane(plane, 1)
-
-    loads[4].wait()
-    loads[7].wait()
-    gather_pairs(compositions, partners, table, parts, pair)
+    stencil(
+        cells, halo, diffusion, fields, blend, scaled, field_table, rows_x, rows_y
+    )
+
+    def go_far(k, _):
+        fill(far_plane(k))
+        send_go(far_plane(k), 0)
+        return 0
+
+    lax.fori_loop(per_section, planes, go_far, 0)
+    gather_pairs(compositions, partners, table, parts, pair, soon, rounds)
     loads[5].wait()
 
     def wait_rates(k, _):
@@ -368,14 +425,12 @@
     lax.fori_loop(0, blocks, weigh, 0, unroll=4)
 
     per = left1.shape[1]
-    wide = acc1.shape[0] // ROWS
-
-    def sum_slots(part, last):
+
+    def sum_slots(section):
         acc1[...] = jnp.zeros(acc1.shape, F32)
 
         def scatter(k, _):
-            rows = [slots[pl.ds(k * (per // LANES) + i, 1), :] for i in range(per // LANES)]
-            group = (jnp.concatenate(rows, 1) >> 8) - part * (wide // 2)
+            group = (row_block(slots, k, per) >> 8) - section * (wide // 2)
             cols = pl.ds(pl.multiple_of(k * per, per), per)
             scatter_block(
                 group, hot1[:, cols], high[:, cols], low[:, cols], left1, acc1, wide // 2
@@ -384,40 +439,67 @@
 
         lax.fori_loop(0, blocks * LANES // per, scatter, 0)
         for i in range(wide):
-            moments[part * wide + i] = acc_row(acc1, i)
-        inside = lax.rem(me, wide)
-
-        def body(i, _):
-            d = part * wide + lax.rem(inside + i, wide)
-            copy_of(*back, me, d, d).start()
+            moments[section * wide + i] = acc_row(acc1, i)
+
+    def send_back(section, first, last):
+        def body(k, _):
+            d = peer(section, k)
+            back_copy(me, d, d).start()
             return 0
 
-        lax.fori_loop(last, wide, body, 0)
-
-    own = lax.div(me, wide)
-
-    def other(k, _):
-        sum_slots(lax.rem(own + k, tiles // wide), 0)
-        return 0
-
-    lax.fori_loop(1, tiles // wide, other, 0)
-    sum_slots(own, 1)
+        lax.fori_loop(first, last, body, 0)
+
+    def other(r, _):
+        section = lax.rem(own + r, sections)
+        sum_slots(section)
+        send_back(section, 0, wide)
+        return 0
+
+    lax.fori_loop(1, sections, other, 0)
+
+    def go_near(k, _):
+        there = own * per_section + lax.rem(plane + k, per_section)
+        fill(there)
+        send_go(there, 0)
+        return 0
+
+    lax.fori_loop(1, per_section, go_near, 0)
+    fill(plane)
+    received[me] = outgoing[me]
+    send_go(plane, 1)
+    sum_slots(own)
+    send_back(own, 0, wide - PLANE)
+    send_back(own, wide - PLANE + 1, wide)
     returned[me] = moments[me]
 
     def wait_go(k, _):
         s = lax.rem(me + k, tiles)
-        copy_of(*go, s, s, s).wait_recv()
+        go_copy(s, s, s).wait_recv()
         return 0
 
     lax.fori_loop(1, tiles, wait_go, 0)
-    add_fields(received, slots, hot1, field_table, field_parts, new)
+    add_fields(received, slots, hot1, table, parts, new)
+
+    for i in range(4):
+
+        @pl.when(sends[i])
+        def _(i=i):
+            halo_copy(i).wait_send()
+
+    def sent(k, _):
+        d = lax.rem(me + k, tiles)
+        rate_copy(me, d, d).wait_send()
+        go_copy(me, d, d).wait_send()
+        return 0
+
+    lax.fori_loop(1, tiles, sent, 0)
 
     acc2[...] = jnp.zeros(acc2.shape, F32)
 
     def collect(there, first):
         def body(i, _):
             s = there * PLANE + lax.rem(inner + i, PLANE)
-            copy_of(*back, s, s, s).wait_recv()
+            back_copy(s, s, s).wait_recv()
             return 0
 
         lax.fori_loop(first, PLANE, body, 0)
@@ -426,33 +508,37 @@
         index = jnp.concatenate([lists[pl.ds(s, 1), :] for s in at], 1)
         top = values.astype(BF16)
         rest = (values - top.astype(F32)).astype(BF16)
-        scatter_block(index >> 8, hot_rows(index), top, rest, left2, acc2, count // 2)
+        cols = pl.ds(pl.multiple_of(there * (PLANE * LANES), PLANE * LANES), PLANE * LANES)
+        scatter_block(index >> 8, hot2[:, cols], top, rest, left2, acc2, count // 2)
 
     collect(plane, 1)
-    lax.fori_loop(
-        1, planes, lambda k, _: (collect(lax.rem(plane + k, planes), 0), 0)[1], 0
-    )
+    near = own * per_section
+
+    def collect_near(k, _):
+        collect(near + lax.rem(plane + k, per_section), 0)
+        return 0
+
+    lax.fori_loop(1, per_section, collect_near, 0)
+
+    def collect_far(k, _):
+        collect(far_plane(k), 0)
+        return 0
+
+    lax.fori_loop(per_section, planes - 1, collect_far, 0)
+
+    def finish(k, _):
+        d = lax.rem(me + k, tiles)
+        back_copy(me, d, d).wait_send()
+        return 0
+
+    lax.fori_loop(1, tiles, finish, 0)
+    collect(far_plane(planes - 1), 0)
     for j in range(count):
         total = acc_row(acc2, j)
         weight = total[species : species + 1]
         mixed = scaled[j, 0:species, :] * weight
-        mean = (total[:species] + mixed + fields[j, 0:species, :]) / (weight + 1.0)
-        out[pl.ds(j, species, stride=count), :] = mean
-
-    for i in range(4):
-
-        @pl.when(sends[i])
-        def _(i=i):
-            halo_copy(i).wait_send()
-
-    def finish(k, _):
-        d = lax.rem(me + k, tiles)
-        rate_copy(me, d, d).wait_send()
-        copy_of(*go, me, d, d).wait_send()
-        copy_of(*back, me, d, d).wait_send()
-        return 0
-
-    lax.fori_loop(1, tiles, finish, 0)
+        mean = total[:species] + mixed + fields[j, 0:species, :]
+        out[pl.ds(j, species, stride=count), :] = mean * (1.0 / (weight + 1.0))
 
 
 def hand_over(first, second, first_out, second_out, sems):
@@ -511,15 +597,15 @@
             vmem(tiles, ROWS, LANES),
             vmem(tiles, ROWS, LANES),
             half_vmem(particles // 256 * ROWS, 512),
-            vmem(particles // 256 * ROWS, 256),
+            vmem(particles // 256 * ROWS, WIDE),
             vmem(ROWS, particles),
             half_vmem(ROWS, particles),
             half_vmem(ROWS, particles),
             half_vmem(256, particles),
+            half_vmem(256, tiles * LANES),
             half_vmem(2 * PLANE * ROWS, 1024),
             vmem(2 * PLANE * ROWS, 256),
-            half_vmem(tiles // 2 * ROWS, 512),
-            vmem(tiles // 2 * ROWS, 256),
+            half_vmem(count // 2 * ROWS, 512),
             half_vmem(count * ROWS, PLANE * LANES),
             vmem(count * ROWS, 256),
             pltpu.SemaphoreType.DMA((8,)),
@@ -531,6 +617,7 @@
             pltpu.SemaphoreType.DMA((tiles,)),
             pltpu.SemaphoreType.DMA((tiles,)),
             pltpu.SemaphoreType.DMA((tiles,)),
+            pltpu.SemaphoreType.REGULAR,
         ],
         compiler_params=pltpu.CompilerParams(
             collective_id=0, has_side_effects=True, vmem_limit_bytes=63 * 1024 * 1024

time: 41.6 us -> 37.5 us (0.901)
  Pallas kernels: 40.7 us -> 36.4 us
    pallas_call x1, Pallas kernels: 39.8 us -> 35.5 us  [on_device(): pl.pallas_call(functools.partial(whole_kernel, lax.axis_size('gx'), lax.a...]
where the time goes in v2:
time: 37.5 us; the launch traced here: 37 us
  Pallas kernels  36.4 us (97%)
  between operations  0.64 us (2%)
    pallas_call x1, Pallas kernels, on_device(): pl.pallas_call(functools.partial(whole_kernel, lax.axis_size('gx'), lax.a...  35.5 us
    pallas_call x1, Pallas kernels, on_device(): pl.pallas_call(hand_over, out_shape=tuple((jax.ShapeDtypeStruct(a.shape,...  0.89 us

profile of v2, /device:TPU:0, one launch (start us, length us, event | category | flops | bytes accessed | tf_op | source)
XLA Modules:
  0.0 37.0 jit_solution(651606980946690115)
XLA Ops:
  0.6 35.5 %whole_kernel.1 = (f32[480,128]{1,0:T(8,128)S(1)}, f32[30,4096]{1,0:T(8,128)S(1)}) custom-call(f32[480,128]{1,0:T(8,128)} %bitcast.8, f32[16,128]{1,0:T(8,128)} %bitcast.13, f32[16,128]{1,0:T(8,128)} %bitcast.14, s32[32,128]{1,0:T(8,128)} %bitcast.9, f32[30,4096]{1,0:T(8,128)} %refs_4_.1, f32[32,128]{1,0:T(8,128)} %bitcast.10, s32[32,128]{1,0:T(8,128)} %bitcast.11, ...), custom_call_target="tpu_custom_call" | custom-call | tf_op jit(solution)/shard_map/whole_kernel/pallas_call | solution.py:575
  36.1 0.9 %hand_over.1 = (f32[480,128]{1,0:T(8,128)}, f32[30,4096]{1,0:T(8,128)}) custom-call(f32[480,128]{1,0:T(8,128)S(1)} %get-tuple-element.6.first, f32[30,4096]{1,0:T(8,128)S(1)} %get-tuple-element.7.second), custom_call_target="tpu_custom_call" | custom-call | tf_op jit(solution)/shard_map/hand_over/pallas_call | solution.py:626

commit v3 on v2

--- a/solution.py
+++ b/solution.py
@@ -14,6 +14,7 @@
 PLANE = 8
 WIDE = 1024
 FIRST = 0
+LAST = 4
 HALO_ROUNDS = 2
 F32 = jnp.float32
 BF16 = jnp.bfloat16
@@ -154,32 +155,29 @@
         out[b : b + 8, :] = total
 
 
-def add_fields(received, slots, hot, table, parts, new):
+def add_fields(received, slots, hot, table, parts, new, section, groups):
     species, particles = new.shape
-    groups = table.shape[0] // ROWS
-
-    def chunk(c, _):
-        for h in range(groups):
-            s = 2 * (c * groups + h)
-            values = jnp.concatenate([received[s], received[s + 1]], 1)
-            first = values.astype(BF16)
-            rows = slice(h * ROWS, (h + 1) * ROWS)
-            table[rows, 0:256] = first
-            table[rows, 256:512] = (values - first.astype(F32)).astype(BF16)
-
-        def body(k, _):
-            at = pl.ds(pl.multiple_of(k * WIDE, WIDE), WIDE)
-            both = hot[:, at]
-            parts[...] = jnp.dot(
-                table[...], jnp.concatenate([both, both], 0), preferred_element_type=F32
-            )
-            index = row_block(slots, k, WIDE) - c * (groups * 256)
-            new[:, at] += select_group(index, parts, groups)[:species]
-            return 0
-
-        return lax.fori_loop(0, particles // WIDE, body, 0)
-
-    lax.fori_loop(0, received.shape[0] // 2 // groups, chunk, 0)
+    for h in range(groups):
+        s = 2 * (section * groups + h)
+        values = jnp.concatenate([received[s], received[s + 1]], 1)
+        first = values.astype(BF16)
+        rows = slice(h * ROWS, (h + 1) * ROWS)
+        table[rows, 0:256] = first
+        table[rows, 256:512] = (values - first.astype(F32)).astype(BF16)
+
+    def body(k, _):
+        at = pl.ds(pl.multiple_of(k * WIDE, WIDE), WIDE)
+        both = hot[:, at]
+        parts[0 : groups * ROWS, :] = jnp.dot(
+            table[0 : groups * ROWS, :],
+            jnp.concatenate([both, both], 0),
+            preferred_element_type=F32,
+        )
+        index = row_block(slots, k, WIDE) - section * (groups * 256)
+        new[:, at] += select_group(index, parts, groups)[:species]
+        return 0
+
+    lax.fori_loop(0, particles // WIDE, body, 0)
 
 
 def whole_kernel(
@@ -248,16 +246,6 @@
             cells[x, y, 0:species, :] = means[pl.ds(j, species, stride=count), :]
             cells[x, y, species:ROWS, :] = jnp.zeros((ROWS - species, LANES), F32)
 
-    rounds = blocks * LANES // WIDE
-    hops = lax.div(gx, 2) + lax.rem(gx, 2) + lax.div(gy, 2)
-    early = jnp.where(hops == 0, FIRST, 0)
-    early = jnp.minimum(early, rounds)
-    soon = jnp.minimum(early + HALO_ROUNDS, rounds)
-    loads[4].wait()
-    loads[7].wait()
-    split_table(compositions, table)
-    gather_pairs(compositions, partners, table, parts, pair, 0, early)
-
     pl.semaphore_wait(barrier, (plane + 1) * PLANE - 1 + above.astype(jnp.int32))
 
     def halo_copy(i):
@@ -278,7 +266,7 @@
 
     sends = (gx < nx - 1, gx > 0, gy < ny - 1, gy > 0)
     receives = (gx > 0, gx < nx - 1, gy > 0, gy < ny - 1)
-    for i in range(4):
+    for i in (2, 3, 0, 1):
 
         @pl.when(sends[i])
         def _(i=i):
@@ -291,6 +279,16 @@
         @pl.when(jnp.logical_not(receives[i]))
         def _(i=i):
             halo[i, :, 0:species] = jnp.zeros(halo[i, :, 0:species].shape, F32)
+
+    rounds = blocks * LANES // WIDE
+    hops = lax.div(gx, 2) + lax.rem(gx, 2) + lax.div(gy, 2)
+    early = jnp.where(hops == 0, FIRST, 0)
+    early = jnp.minimum(early, rounds)
+    soon = jnp.minimum(early + HALO_ROUNDS, rounds)
+    loads[4].wait()
+    loads[7].wait()
+    split_table(compositions, table)
+    gather_pairs(compositions, partners, table, parts, pair, 0, early)
 
     loads[2].wait()
     loads[3].wait()
@@ -472,13 +470,56 @@
     send_back(own, wide - PLANE + 1, wide)
     returned[me] = moments[me]
 
-    def wait_go(k, _):
-        s = lax.rem(me + k, tiles)
+    def wait_go(s, _):
         go_copy(s, s, s).wait_recv()
         return 0
 
-    lax.fori_loop(1, tiles, wait_go, 0)
-    add_fields(received, slots, hot1, table, parts, new)
+    def add_section(section):
+        add_fields(received, slots, hot1, table, parts, new, section, wide // 2)
+
+    lax.fori_loop(own * wide, me, wait_go, 0)
+    lax.fori_loop(me + 1, (own + 1) * wide, wait_go, 0)
+    add_section(own)
+    acc2[...] = jnp.zeros(acc2.shape, F32)
+
+    def wait_back(there, first, last):
+        def body(i, _):
+            s = there * PLANE + i
+            back_copy(s, s, s).wait_recv()
+            return 0
+
+        lax.fori_loop(first, last, body, 0)
+
+    def collect(there, first, many):
+        at = [there * PLANE + first + i for i in range(many)]
+        values = jnp.concatenate([returned[s] for s in at], 1)
+        index = jnp.concatenate([lists[pl.ds(s, 1), :] for s in at], 1)
+        top = values.astype(BF16)
+        rest = (values - top.astype(F32)).astype(BF16)
+        start = there * (PLANE * LANES) + first * LANES
+        cols = pl.ds(pl.multiple_of(start, many * LANES), many * LANES)
+        left = left2.at[:, 0 : many * LANES]
+        scatter_block(index >> 8, hot2[:, cols], top, rest, left, acc2, count // 2)
+
+    wait_back(plane, 0, inner)
+    wait_back(plane, inner + 1, PLANE)
+    collect(plane, 0, PLANE)
+    near = own * per_section
+
+    def collect_near(k, _):
+        there = near + lax.rem(plane + k, per_section)
+        wait_back(there, 0, PLANE)
+        collect(there, 0, PLANE)
+        return 0
+
+    lax.fori_loop(1, per_section, collect_near, 0)
+    def add_far(r, _):
+        section = lax.rem(own + r, sections)
+        lax.fori_loop(section * wide, (section + 1) * wide, wait_go, 0)
+        add_section(section)
+        return 0
+
+    lax.fori_loop(1, sections, add_far, 0)
 
     for i in range(4):
 
@@ -494,51 +535,37 @@
 
     lax.fori_loop(1, tiles, sent, 0)
 
-    acc2[...] = jnp.zeros(acc2.shape, F32)
-
-    def collect(there, first):
-        def body(i, _):
-            s = there * PLANE + lax.rem(inner + i, PLANE)
-            back_copy(s, s, s).wait_recv()
-            return 0
-
-        lax.fori_loop(first, PLANE, body, 0)
-        at = [there * PLANE + i for i in range(PLANE)]
-        values = jnp.concatenate([returned[s] for s in at], 1)
-        index = jnp.concatenate([lists[pl.ds(s, 1), :] for s in at], 1)
-        top = values.astype(BF16)
-        rest = (values - top.astype(F32)).astype(BF16)
-        cols = pl.ds(pl.multiple_of(there * (PLANE * LANES), PLANE * LANES), PLANE * LANES)
-        scatter_block(index >> 8, hot2[:, cols], top, rest, left2, acc2, count // 2)
-
-    collect(plane, 1)
-    near = own * per_section
-
-    def collect_near(k, _):
-        collect(near + lax.rem(plane + k, per_section), 0)
-        return 0
-
-    lax.fori_loop(1, per_section, collect_near, 0)
+    reverse = own < (sections + 1) // 2
+
+    def far_back(k):
+        return far_plane(jnp.where(reverse, planes - 1 + per_section - k, k))
 
     def collect_far(k, _):
-        collect(far_plane(k), 0)
+        wait_back(far_back(k), 0, PLANE)
+        collect(far_back(k), 0, PLANE)
         return 0
 
     lax.fori_loop(per_section, planes - 1, collect_far, 0)
+    last = far_back(planes - 1)
+    half = lax.div(lax.rem(inner + 1, PLANE), LAST)
+    for part in range(PLANE // LAST):
+        first = lax.rem(half + 1 + part, PLANE // LAST) * LAST
+        wait_back(last, first, first + LAST)
+        collect(last, first, LAST)
 
     def finish(k, _):
         d = lax.rem(me + k, tiles)
         back_copy(me, d, d).wait_send()
         return 0
 
-    lax.fori_loop(1, tiles, finish, 0)
-    collect(far_plane(planes - 1), 0)
     for j in range(count):
         total = acc_row(acc2, j)
         weight = total[species : species + 1]
         mixed = scaled[j, 0:species, :] * weight
         mean = total[:species] + mixed + fields[j, 0:species, :]
         out[pl.ds(j, species, stride=count), :] = mean * (1.0 / (weight + 1.0))
+
+    lax.fori_loop(1, tiles, finish, 0)
 
 
 def hand_over(first, second, first_out, second_out, sems):

time: 37.5 us -> 36.2 us (0.965)
  Pallas kernels: 36.4 us -> 35.4 us
    pallas_call x1, Pallas kernels: 35.5 us -> 34.5 us  [on_device(): pl.pallas_call(functools.partial(whole_kernel, lax.axis_size('gx'), lax.a...]
where the time goes in v3:
time: 36.2 us; the launch traced here: 36 us
  Pallas kernels  35.4 us (98%)
  between operations  0.64 us (2%)
    pallas_call x1, Pallas kernels, on_device(): pl.pallas_call(functools.partial(whole_kernel, lax.axis_size('gx'), lax.a...  34.5 us
    pallas_call x1, Pallas kernels, on_device(): pl.pallas_call(hand_over, out_shape=tuple((jax.ShapeDtypeStruct(a.shape,...  0.89 us

profile of v3, /device:TPU:0, one launch (start us, length us, event | category | flops | bytes accessed | tf_op | source)
XLA Modules:
  0.0 36.0 jit_solution(3528842548121276341)
XLA Ops:
  0.6 34.5 %whole_kernel.1 = (f32[480,128]{1,0:T(8,128)S(1)}, f32[30,4096]{1,0:T(8,128)S(1)}) custom-call(f32[480,128]{1,0:T(8,128)} %bitcast.8, f32[16,128]{1,0:T(8,128)} %bitcast.13, f32[16,128]{1,0:T(8,128)} %bitcast.14, s32[32,128]{1,0:T(8,128)} %bitcast.9, f32[30,4096]{1,0:T(8,128)} %refs_4_.1, f32[32,128]{1,0:T(8,128)} %bitcast.10, s32[32,128]{1,0:T(8,128)} %bitcast.11, ...), custom_call_target="tpu_custom_call" | custom-call | tf_op jit(solution)/shard_map/whole_kernel/pallas_call | solution.py:602
  35.1 0.9 %hand_over.1 = (f32[480,128]{1,0:T(8,128)}, f32[30,4096]{1,0:T(8,128)}) custom-call(f32[480,128]{1,0:T(8,128)S(1)} %get-tuple-element.6.first, f32[30,4096]{1,0:T(8,128)S(1)} %get-tuple-element.7.second), custom_call_target="tpu_custom_call" | custom-call | tf_op jit(solution)/shard_map/hand_over/pallas_call | solution.py:653

commit v4 on v3

--- a/solution.py
+++ b/solution.py
@@ -15,7 +15,7 @@
 WIDE = 1024
 FIRST = 0
 LAST = 4
-HALO_ROUNDS = 2
+HALO_ROUNDS = 1
 F32 = jnp.float32
 BF16 = jnp.bfloat16
 
@@ -33,20 +33,32 @@
     return jnp.concatenate([table[pl.ds(k * many + i, 1), :] for i in range(many)], 1)
 
 
-def stencil(cells, halo, diffusion, fields, blend, scaled, table, rows_x, rows_y):
+def inside(cells, diffusion, fields, rows_x, rows_y):
     lane = lax.broadcasted_iota(jnp.int32, (ROWS, LANES), 1)
     for x in range(rows_x):
         for y in range(rows_y):
             mid = cells[x, y]
-            total = cells[x + 1, y] if x + 1 < rows_x else halo[1, y]
-            total = total + (cells[x - 1, y] if x else halo[0, y])
-            total = total + (cells[x, y + 1] if y + 1 < rows_y else halo[3, x])
-            total = total + (cells[x, y - 1] if y else halo[2, x])
-            total = total + jnp.where(lane < LANES - 1, pltpu.roll(mid, LANES - 1, 1), 0.0)
+            total = jnp.where(lane < LANES - 1, pltpu.roll(mid, LANES - 1, 1), 0.0)
             total = total + jnp.where(lane > 0, pltpu.roll(mid, 1, 1), 0.0)
+            for other in ((x + 1, y), (x - 1, y), (x, y + 1), (x, y - 1)):
+                if 0 <= other[0] < rows_x and 0 <= other[1] < rows_y:
+                    total = total + cells[other[0], other[1]]
             j = x * rows_y + y
-            filtered = mid + diffusion[j : j + 1, :] * (total - 6.0 * mid)
-            fields[j] = filtered
+            fields[j] = mid + diffusion[j : j + 1, :] * (total - 6.0 * mid)
+
+
+def rim(halo, diffusion, fields, blend, scaled, table, rows_x, rows_y):
+    for x in range(rows_x):
+        for y in range(rows_y):
+            j = x * rows_y + y
+            outer = [halo[1, y]] if x + 1 == rows_x else []
+            outer += [halo[0, y]] if x == 0 else []
+            outer += [halo[3, x]] if y + 1 == rows_y else []
+            outer += [halo[2, x]] if y == 0 else []
+            filtered = fields[j]
+            if outer:
+                filtered = filtered + diffusion[j : j + 1, :] * sum(outer[1:], outer[0])
+                fields[j] = filtered
             mixed = filtered * blend[j : j + 1, :]
             scaled[j] = mixed
             first = mixed.astype(BF16)
@@ -318,6 +330,7 @@
     for b in range(0, tiles, 4):
         hot2[:, b * LANES : (b + 4) * LANES] = hot_rows(row_block(lists, b // 4, 4 * LANES))
     loads[1].wait()
+    inside(cells, diffusion, fields, rows_x, rows_y)
     gather_pairs(compositions, partners, table, parts, pair, early, soon)
 
     @pl.when(plane < planes - 1)
@@ -385,17 +398,26 @@
         def _(i=i):
             halo_copy(i).wait_recv()
 
-    stencil(
-        cells, halo, diffusion, fields, blend, scaled, field_table, rows_x, rows_y
-    )
+    rim(halo, diffusion, fields, blend, scaled, field_table, rows_x, rows_y)
 
     def go_far(k, _):
         fill(far_plane(k))
         send_go(far_plane(k), 0)
         return 0
 
-    lax.fori_loop(per_section, planes, go_far, 0)
+    lax.fori_loop(per_section, planes - 1, go_far, 0)
     gather_pairs(compositions, partners, table, parts, pair, soon, rounds)
+    lax.fori_loop(planes - 1, planes, go_far, 0)
+    def go_near(k, _):
+        there = own * per_section + lax.rem(plane + k, per_section)
+        fill(there)
+        send_go(there, 0)
+        return 0
+
+    lax.fori_loop(1, per_section, go_near, 0)
+    fill(plane)
+    received[me] = outgoing[me]
+    send_go(plane, 1)
     loads[5].wait()
 
     def wait_rates(k, _):
@@ -455,16 +477,6 @@
 
     lax.fori_loop(1, sections, other, 0)
 
-    def go_near(k, _):
-        there = own * per_section + lax.rem(plane + k, per_section)
-        fill(there)
-        send_go(there, 0)
-        return 0
-
-    lax.fori_loop(1, per_section, go_near, 0)
-    fill(plane)
-    received[me] = outgoing[me]
-    send_go(plane, 1)
     sum_slots(own)
     send_back(own, 0, wide - PLANE)
     send_back(own, wide - PLANE + 1, wide)
@@ -548,15 +560,25 @@
     lax.fori_loop(per_section, planes - 1, collect_far, 0)
     last = far_back(planes - 1)
     half = lax.div(lax.rem(inner + 1, PLANE), LAST)
+
+    def finish(d, _):
+        back_copy(me, d, d).wait_send()
+        return 0
+
+    def finish_plane(there):
+        lax.fori_loop(there * PLANE, (there + 1) * PLANE, finish, 0)
+
+    def finish_far(k, _):
+        finish_plane(far_plane(k))
+        return 0
+
+    lax.fori_loop(per_section, planes - 1, finish_far, 0)
+    lax.fori_loop(own * wide, me, finish, 0)
+    lax.fori_loop(me + 1, (own + 1) * wide, finish, 0)
     for part in range(PLANE // LAST):
         first = lax.rem(half + 1 + part, PLANE // LAST) * LAST
         wait_back(last, first, first + LAST)
         collect(last, first, LAST)
-
-    def finish(k, _):
-        d = lax.rem(me + k, tiles)
-        back_copy(me, d, d).wait_send()
-        return 0
 
     for j in range(count):
         total = acc_row(acc2, j)
@@ -565,7 +587,7 @@
         mean = total[:species] + mixed + fields[j, 0:species, :]
         out[pl.ds(j, species, stride=count), :] = mean * (1.0 / (weight + 1.0))
 
-    lax.fori_loop(1, tiles, finish, 0)
+    finish_plane(far_plane(planes - 1))
 
 
 def hand_over(first, second, first_out, second_out, sems):

time: 36.2 us -> 35.5 us (0.981)
  Pallas kernels: 35.4 us -> 34.7 us
    pallas_call x1, Pallas kernels: 34.5 us -> 33.9 us  [on_device(): pl.pallas_call(functools.partial(whole_kernel, lax.axis_size('gx'), lax.a...]
where the time goes in v4:
time: 35.5 us; the launch traced here: 35.4 us
  Pallas kernels  34.7 us (98%)
  between operations  0.64 us (2%)
    pallas_call x1, Pallas kernels, on_device(): pl.pallas_call(functools.partial(whole_kernel, lax.axis_size('gx'), lax.a...  33.9 us
    pallas_call x1, Pallas kernels, on_device(): pl.pallas_call(hand_over, out_shape=tuple((jax.ShapeDtypeStruct(a.shape,...  0.89 us

profile of v4, /device:TPU:0, one launch (start us, length us, event | category | flops | bytes accessed | tf_op | source)
XLA Modules:
  0.0 35.4 jit_solution(10382507325897508168)
XLA Ops:
  0.6 33.9 %whole_kernel.1 = (f32[480,128]{1,0:T(8,128)S(1)}, f32[30,4096]{1,0:T(8,128)S(1)}) custom-call(f32[480,128]{1,0:T(8,128)} %bitcast.8, f32[16,128]{1,0:T(8,128)} %bitcast.13, f32[16,128]{1,0:T(8,128)} %bitcast.14, s32[32,128]{1,0:T(8,128)} %bitcast.9, f32[30,4096]{1,0:T(8,128)} %refs_4_.1, f32[32,128]{1,0:T(8,128)} %bitcast.10, s32[32,128]{1,0:T(8,128)} %bitcast.11, ...), custom_call_target="tpu_custom_call" | custom-call | tf_op jit(solution)/shard_map/whole_kernel/pallas_call | solution.py:624
  34.5 0.9 %hand_over.1 = (f32[480,128]{1,0:T(8,128)}, f32[30,4096]{1,0:T(8,128)}) custom-call(f32[480,128]{1,0:T(8,128)S(1)} %get-tuple-element.6.first, f32[30,4096]{1,0:T(8,128)S(1)} %get-tuple-element.7.second), custom_call_target="tpu_custom_call" | custom-call | tf_op jit(solution)/shard_map/hand_over/pallas_call | solution.py:675

commit v5 on v4

--- a/solution.py
+++ b/solution.py
@@ -47,7 +47,7 @@
             fields[j] = mid + diffusion[j : j + 1, :] * (total - 6.0 * mid)
 
 
-def rim(halo, diffusion, fields, blend, scaled, table, rows_x, rows_y):
+def rim(halo, diffusion, fields, blend, table, rows_x, rows_y):
     for x in range(rows_x):
         for y in range(rows_y):
             j = x * rows_y + y
@@ -60,7 +60,6 @@
                 filtered = filtered + diffusion[j : j + 1, :] * sum(outer[1:], outer[0])
                 fields[j] = filtered
             mixed = filtered * blend[j : j + 1, :]
-            scaled[j] = mixed
             first = mixed.astype(BF16)
             rows = slice(j // 2 * ROWS, (j // 2 + 1) * ROWS)
             at = j % 2 * LANES
@@ -199,7 +198,7 @@
     staged, refs = refs[:8], refs[8:]
     means, diffusion, rate, lists, compositions, weights, slots, partners = staged
     (
-        cells, halo, fields, scaled, rates_out, rates_in, rates, outgoing, received, moments,
+        cells, halo, fields, rates_out, rates_in, rates, outgoing, received, moments,
         returned, table, parts, pair, high, low, hot1, hot2, left1, acc1, field_table, left2, acc2,
         in_sems, halo_send, halo_recv, rate_send, rate_recv, go_send, go_recv,
         back_send, back_recv, late,
@@ -398,7 +397,7 @@
         def _(i=i):
             halo_copy(i).wait_recv()
 
-    rim(halo, diffusion, fields, blend, scaled, field_table, rows_x, rows_y)
+    rim(halo, diffusion, fields, blend, field_table, rows_x, rows_y)
 
     def go_far(k, _):
         fill(far_plane(k))
@@ -406,8 +405,8 @@
         return 0
 
     lax.fori_loop(per_section, planes - 1, go_far, 0)
+    lax.fori_loop(planes - 1, planes, go_far, 0)
     gather_pairs(compositions, partners, table, parts, pair, soon, rounds)
-    lax.fori_loop(planes - 1, planes, go_far, 0)
     def go_near(k, _):
         there = own * per_section + lax.rem(plane + k, per_section)
         fill(there)
@@ -583,8 +582,7 @@
     for j in range(count):
         total = acc_row(acc2, j)
         weight = total[species : species + 1]
-        mixed = scaled[j, 0:species, :] * weight
-        mean = total[:species] + mixed + fields[j, 0:species, :]
+        mean = total[:species] + fields[j, 0:species, :] * (blend[j : j + 1, :] * weight + 1.0)
         out[pl.ds(j, species, stride=count), :] = mean * (1.0 / (weight + 1.0))
 
     finish_plane(far_plane(planes - 1))
@@ -636,7 +634,6 @@
         + [
             vmem(rows_x, rows_y, ROWS, LANES),
             vmem(4, max(rows_x, rows_y), ROWS, LANES),
-            vmem(count, ROWS, LANES),
             vmem(count, ROWS, LANES),
             vmem(tiles, 1, LANES),
             vmem(tiles, 1, LANES),

time: 35.5 us -> 35.5 us (level)
  no operation moved by 1% of the time
where the time goes in v5:
time: 35.5 us; the launch traced here: 35.4 us
  Pallas kernels  34.7 us (98%)
  between operations  0.64 us (2%)
    pallas_call x1, Pallas kernels, on_device(): pl.pallas_call(functools.partial(whole_kernel, lax.axis_size('gx'), lax.a...  33.8 us
    pallas_call x1, Pallas kernels, on_device(): pl.pallas_call(hand_over, out_shape=tuple((jax.ShapeDtypeStruct(a.shape,...  0.89 us

profile of v5, /device:TPU:0, one launch (start us, length us, event | category | flops | bytes accessed | tf_op | source)
XLA Modules:
  0.0 35.4 jit_solution(9948271161582872997)
XLA Ops:
  0.6 33.8 %whole_kernel.1 = (f32[480,128]{1,0:T(8,128)S(1)}, f32[30,4096]{1,0:T(8,128)S(1)}) custom-call(f32[480,128]{1,0:T(8,128)} %bitcast.8, f32[16,128]{1,0:T(8,128)} %bitcast.13, f32[16,128]{1,0:T(8,128)} %bitcast.14, s32[32,128]{1,0:T(8,128)} %bitcast.9, f32[30,4096]{1,0:T(8,128)} %refs_4_.1, f32[32,128]{1,0:T(8,128)} %bitcast.10, s32[32,128]{1,0:T(8,128)} %bitcast.11, ...), custom_call_target="tpu_custom_call" | custom-call | tf_op jit(solution)/shard_map/whole_kernel/pallas_call | solution.py:622
  34.5 0.9 %hand_over.1 = (f32[480,128]{1,0:T(8,128)}, f32[30,4096]{1,0:T(8,128)}) custom-call(f32[480,128]{1,0:T(8,128)S(1)} %get-tuple-element.6.first, f32[30,4096]{1,0:T(8,128)S(1)} %get-tuple-element.7.second), custom_call_target="tpu_custom_call" | custom-call | tf_op jit(solution)/shard_map/hand_over/pallas_call | solution.py:672
